TPU v7x, 32 devices: a whole 2x2x4 slice. The times are simulated.
32 devices in a mesh: groups: 2 (over y), sol: 4 (over z), head: 2 (over x), sub: 2 (over core).
Axes of the slice: x: 2, y: 2, z: 4, core: 2. Of those that a mesh axis runs over, the one named last changes fastest.
Arguments:
- query_key: bfloat16 [16, 512, 2, 2048], P(('groups', 'sol'), None, None, ('head', 'sub')), parts along dimension 0, may hold values from -6 to 6
- values_in: bfloat16 [16, 512, 4096], P(('groups', 'sol'), None, ('head', 'sub')), parts along dimension 0, may hold values from -6 to 6
- gate_in: bfloat16 [16, 512, 4096], P(('groups', 'sol'), None, ('head', 'sub')), parts along dimension 0, may hold values from -6 to 6
- decay_in: float32 [16, 32, 512], P(('groups', 'sol'), ('head', 'sub')), parts along dimension 0, may hold values from -6 to 6
- beta_in: float32 [16, 32, 512], P(('groups', 'sol'), ('head', 'sub')), parts along dimension 0, may hold values from -6 to 6
- decay_rate: float32 [32], P(('head', 'sub')), may hold values from 0.002 to 0.08
- decay_bias: float32 [32], P(('head', 'sub')), may hold values from -1 to 1
- conv_qk: float32 [4, 2, 2048], P(None, None, ('head', 'sub')), may hold values from -3 to 3
- conv_v: float32 [4, 4096], P(None, ('head', 'sub')), may hold values from -3 to 3
- prompt_states: bfloat16 [8, 32, 128, 128], P(('groups', 'sol'), ('head', 'sub')), parts along dimension 0, may hold values from -6 to 6
- prompt_of: int32 [16], P(('groups', 'sol')), parts along dimension 0, may hold values from 0 to 3
- step_ends: int32 [16, 2], P(('groups', 'sol')), parts along dimension 0, may hold values from 1 to 512, as said below
- norm_gain: float32 [128], replicated, may hold values from 0.25 to 1.75
- probe: bfloat16 [4096], replicated, may hold values from -0.09375 to 0.09375
Outputs:
- hidden: bfloat16 [16, 512, 4096], P(('groups', 'sol'), ('head', 'sub')), parts along dimension 0
- step_logits: float32 [16, 2], P(('groups', 'sol')), parts along dimension 0
There are 2 independent parts, one for each index of `groups`. A program takes and returns all parts, laid end to end along the dimension named above; an argument that names none is the same for every part. Nothing has to cross between parts.
Inputs may be any that keep to these rules, and one draw needn't show every extreme that they name: Solution s continues prompt prompt_of[s]. step_ends[s,0] < step_ends[s,1]; the first step covers positions below step_ends[s,0], the second the positions from there below step_ends[s,1]; later positions are padding. Some solution has step_ends[s,1] = 512.
All inputs are finite; a program needn't handle non-finite values.
Results may differ from a plain program's by a relative error of at most 0.0032.
Values may be sent and summed in bfloat16 or wider, within the bound.
A program may use at most 128 MiB of HBM per device.

v0:
```python
import jax
import jax.numpy as jnp
from jax import lax
from jax.sharding import PartitionSpec as P

BLOCK = 128


def conv_silu(inputs, kernel):
    width = kernel.shape[0]
    count = inputs.shape[1]
    padded = jnp.pad(inputs, ((0, 0), (width - 1, 0), (0, 0)))
    total = jnp.zeros(inputs.shape, jnp.float32)
    for offset in range(width):
        total = total + padded[:, offset : offset + count, :] * kernel[offset]
    return jax.nn.silu(total)


def unit_rows(field, head_size):
    shape = field.shape
    split = field.reshape(shape[:-1] + (shape[-1] // head_size, head_size))
    return split / jnp.sqrt(jnp.sum(split * split, axis=-1, keepdims=True) + 1e-06)


def pick_states(owners, block):
    labels = jnp.arange(block.shape[0], dtype=jnp.int32)
    select = (owners[:, None] == labels[None, :]).astype(jnp.bfloat16)
    return jnp.einsum("sp,phkv->shkv", select, block, preferred_element_type=jnp.float32)


def delta_blocks(queries, keys, values, log_decay, beta, initial):
    sols, length, heads, size = queries.shape
    count = length // BLOCK
    highest = lax.Precision.HIGHEST

    def blocks(field):
        return field.reshape(sols, count, BLOCK, heads, size).transpose(1, 0, 3, 2, 4)

    def gates(field):
        return field.reshape(sols, heads, count, BLOCK).transpose(2, 0, 1, 3)

    query_blocks = blocks(queries)
    key_blocks = blocks(keys)
    value_blocks = blocks(values)
    cumulative = jnp.cumsum(gates(log_decay), axis=-1)
    rate = gates(beta)
    places = jnp.arange(BLOCK)
    within = places[:, None] >= places[None, :]
    strict = places[:, None] > places[None, :]
    spread = cumulative[..., :, None] - cumulative[..., None, :]
    weights = jnp.where(within, jnp.exp(jnp.where(within, spread, 0.0)), 0.0)
    key_gram = jnp.einsum("nshid,nshjd->nshij", key_blocks, key_blocks, precision=highest)
    system = jnp.eye(BLOCK, dtype=jnp.float32) + jnp.where(
        strict, rate[..., :, None] * key_gram * weights, 0.0
    )
    right = jnp.concatenate(
        [rate[..., None] * value_blocks, (rate * jnp.exp(cumulative))[..., None] * key_blocks],
        axis=-1,
    )
    solved = jax.scipy.linalg.solve_triangular(system, right, lower=True, unit_diagonal=True)
    updates = solved[..., :size]
    corrections = solved[..., size:]
    scores = jnp.einsum("nshid,nshjd->nshij", query_blocks, key_blocks, precision=highest) * weights

    def advance(state, inputs):
        query, key, update, correction, score, cumul = inputs
        fresh = update - jnp.einsum("shck,shkv->shcv", correction, state, precision=highest)
        output = jnp.exp(cumul)[..., None] * jnp.einsum(
            "shck,shkv->shcv", query, state, precision=highest
        )
        output = output + jnp.einsum("shij,shjv->shiv", score, fresh, precision=highest)
        last = cumul[..., -1:]
        tail = jnp.exp(last - cumul)
        state = jnp.exp(last)[..., None] * state + jnp.einsum(
            "shck,shcv->shkv", key * tail[..., None], fresh, precision=highest
        )
        return (state, output)

    unused, outputs = lax.scan(
        advance, initial, (query_blocks, key_blocks, updates, corrections, scores, cumulative)
    )
    return outputs.transpose(1, 0, 3, 2, 4).reshape(sols, length, heads * size)


def gated_norm(core, gate, gain, first, ends):
    sols, count, width = core.shape
    size = gain.shape[0]
    split = core.reshape(sols, count, width // size, size)
    scale = jnp.sqrt(jnp.mean(split * split, axis=-1, keepdims=True) + 1e-06)
    normed = split / scale * gain * jax.nn.silu(gate.reshape(split.shape).astype(jnp.float32))
    places = first + jnp.arange(count, dtype=jnp.int32)
    live = places[None, :] < ends[:, 1:2]
    hidden = jnp.where(live[:, :, None], normed.reshape(sols, count, width), 0.0).astype(
        jnp.bfloat16
    )
    return (hidden, places)


def end_terms(hidden, probe_part, places, ends):
    sols, count, width = hidden.shape
    reward = jnp.dot(
        hidden.reshape(sols * count, width), probe_part, preferred_element_type=jnp.float32
    ).reshape(sols, count)
    marked = places[None, :, None] == (ends - 1)[:, None, :]
    return jnp.sum(jnp.where(marked, reward[:, :, None], 0.0), axis=1)


def shuffle_pair(core, gate):
    moved_core, moved_gate = (
        lax.all_to_all(core, ("head", "sub"), split_axis=1, concat_axis=2, tiled=True),
        lax.all_to_all(
            gate.astype(jnp.float32), ("head", "sub"), split_axis=1, concat_axis=2, tiled=True
        ).astype(gate.dtype),
    )
    return (moved_core, moved_gate)


def on_device(
    query_key,
    values_in,
    gate_in,
    decay_in,
    beta_in,
    decay_rate,
    decay_bias,
    conv_qk,
    conv_v,
    prompt_states,
    prompt_of,
    step_ends,
    norm_gain,
    probe,
):
    sols, length = (query_key.shape[0], query_key.shape[1])
    key_width = query_key.shape[3]
    head_size = prompt_states.shape[-1]
    value_heads = prompt_states.shape[1]
    mixed = conv_silu(
        query_key.reshape(sols, length, 2 * key_width),
        conv_qk.reshape(conv_qk.shape[0], 2 * key_width),
    )
    queries = unit_rows(mixed[:, :, :key_width], head_size) * head_size ** (-0.5)
    keys = unit_rows(mixed[:, :, key_width:], head_size)
    repeat = value_heads // queries.shape[2]
    queries = jnp.repeat(queries, repeat, axis=2)
    keys = jnp.repeat(keys, repeat, axis=2)
    values = conv_silu(values_in, conv_v).reshape(sols, length, value_heads, head_size)
    log_decay = -decay_rate[None, :, None] * jax.nn.softplus(decay_in + decay_bias[None, :, None])
    beta = jax.nn.sigmoid(beta_in)
    every = lax.all_gather(prompt_states, "sol", axis=0, tiled=True)
    initial = pick_states(prompt_of, every)
    core = delta_blocks(queries, keys, values, log_decay, beta, initial)
    moved_core, moved_gate = shuffle_pair(core, gate_in)
    share = length // lax.axis_size(("head", "sub"))
    hidden, places = gated_norm(
        moved_core, moved_gate, norm_gain, lax.axis_index(("head", "sub")) * share, step_ends
    )
    partial_value = end_terms(hidden, probe, places, step_ends)
    step_logits = lax.psum(partial_value, ("head", "sub"))
    return (hidden, step_logits)


def solution(mesh):
    return jax.shard_map(
        on_device,
        mesh=mesh,
        in_specs=(
            P(("groups", "sol"), None, None, ("head", "sub")),
            P(("groups", "sol"), None, ("head", "sub")),
            P(("groups", "sol"), None, ("head", "sub")),
            P(("groups", "sol"), ("head", "sub"), None),
            P(("groups", "sol"), ("head", "sub"), None),
            P(("head", "sub")),
            P(("head", "sub")),
            P(None, None, ("head", "sub")),
            P(None, ("head", "sub")),
            P(("groups", "sol"), ("head", "sub"), None, None),
            P(("groups", "sol")),
            P(("groups", "sol"), None),
            P(),
            P(),
        ),
        out_specs=(P(("groups", "sol"), ("head", "sub"), None), P(("groups", "sol"), None)),
        check_vma=False,
    )
```

profile of v0, /device:TPU:0, one launch (start us, length us, event | category | flops | bytes accessed | tf_op | source)
XLA Modules:
  0.0 896.1 jit_solution(11144132423608465836)
XLA Ops:
  7.9 5.1 copy.128
  13.0 4.8 all-to-all-start.1
  17.9 3.3 reshape.201
  21.2 2.8 divide_multiply_fusion.1
  24.0 2.6 fusion.49
  26.5 1.9 reshape.202
  28.5 1.2 multiply_reduce_fusion.1
  29.8 1.4 broadcast_divide_fusion
  31.4 2.8 divide_multiply_fusion
  34.2 2.9 copy.143
  37.3 2.3 reduce_window_sum.11
  40.1 1.9 copy-done.1
  42.1 11.1 %add_bitcast_fusion = f32[4,2,8,1,128,128]{5,4,3,2,1,0:T(8,128)} fusion(f32[128,128]{1,0:T(8,128)S(1)} %get-tuple-element.149, f32[4,2,8,128]{3,2,1,0:T(8,128)S(1)} %reduce_window_sum.11, f32[4,2,8,128]{3,2,1,0:T(8,128)S(1)} %copy_bitcast_fusion, f32[128,128]{1,0:T(8,128)S(1)} %get-tuple-element.148, pred[128,128]{1,0:T(8,128)(4,1)S(1)} %iota_compare_fusion.1, ...), kind=kOutput, calls=%fused_computation.44 | convolution fusion | flops 1620049920 | bytes 8634368 | tf_op jit(solution)/shard_map/nshid,nshjd->nshij/dot_general | solution.py:52
  53.2 630.3 %custom-call.4 = f32[4,2,8,1,128,128]{4,5,3,2,1,0:T(8,128)} custom-call(f32[4,2,8,1,128,128]{5,4,3,2,1,0:T(8,128)} %add_bitcast_fusion), custom_call_target="InvertDiagBlocksLowerTriangular" | custom-call | tf_op jit(solution)/shard_map/jit(_solve_triangular)/vmap(vmap(vmap()))/triangular_solve | solution.py:60
  683.5 2.4 reshape.204
  685.9 1.2 multiply_reduce_fusion
  687.2 1.5 divide_multiply_fusion.2
  689.4 2.0 copy-done.4
  691.4 2.2 copy.122
  693.6 5.2 bitcast_multiply_fusion.3
  698.8 10.3 %fusion.12 = f32[4,2,8,128,256]{4,3,2,1,0:T(8,128)S(1)} fusion(f32[4,2,8,128,128]{4,3,2,1,0:T(8,128)S(1)} %get-tuple-element.151, f32[4,2,8,128,128]{4,3,2,1,0:T(8,128)S(1)} %get-tuple-element.150, f32[4,2,8,1,128,128]{4,5,3,2,1,0:T(8,128)} %custom-call.4), kind=kOutput, calls=%fused_computation.23 | convolution fusion | flops 3223322624 | bytes 20971520 | tf_op jit(solution)/shard_map/jit(_solve_triangular)/vmap(vmap(vmap()))/triangular_solve | solution.py:60
  709.1 5.3 fusion.48
  714.4 1.1 copy-done.5
  715.5 10.6 %fusion.27 = f32[4,2,8,128,128]{4,3,2,1,0:T(8,128)} fusion(f32[4,2,8,128]{3,2,1,0:T(8,128)S(1)} %reduce_window_sum.11, pred[128,128]{1,0:T(8,128)(4,1)S(1)} %iota_compare_fusion.1, f32[2,4,128,8,128]{4,2,1,3,0:T(8,128)S(1)} %bitcast.180, f32[4,2,8,128,128]{4,3,0,2,1:T(8,128)S(1)} %bitcast.185), kind=kOutput, calls=%fused_computation.46 | convolution fusion | flops 1614807040 | bytes 12632064 | tf_op jit(solution)/shard_map/nshid,nshjd->nshij/dot_general | solution.py:63
  726.1 2.2 fusion.35
  728.4 58.6 %while.13 = (s32[]{:T(128)}, f32[2,8,128,128]{3,2,1,0:T(8,128)S(1)}, f32[4,2,8,128,128]{4,3,2,1,0:T(8,128)}, f32[4,2,8,128]{3,2,1,0:T(8,128)S(1)}, f32[4,2,8,128...) while((s32[]{:T(128)}, ...), condition=%wide.region_4.5_spmd.clone, body=%wide.region_3.4_spmd.sunk.clone | while | flops 1612187648 | bytes 20032420 | solution.py:79
  728.8 2.5 convolution_multiply_fusion.3
  731.3 2.8 convolution_subtract_fusion.3
  734.1 3.4 fusion.82
  737.6 2.3 constant_dynamic-slice_fusion.6
  739.9 1.6 copy.174
  741.5 1.6 convolution_add_fusion.4
  743.4 2.5 convolution_multiply_fusion.3
  745.9 2.8 convolution_subtract_fusion.3
  748.7 3.4 fusion.82
  752.2 2.3 constant_dynamic-slice_fusion.6
  754.5 1.6 copy.174
  756.1 1.6 convolution_add_fusion.4
  758.1 2.5 convolution_multiply_fusion.3
  760.6 2.8 convolution_subtract_fusion.3
  763.4 3.4 fusion.82
  766.8 2.3 constant_dynamic-slice_fusion.6
  769.2 1.6 copy.174
  770.7 1.6 convolution_add_fusion.4
  772.7 2.5 convolution_multiply_fusion.3
  775.2 2.8 convolution_subtract_fusion.3
  778.0 3.4 fusion.82
  781.5 2.3 constant_dynamic-slice_fusion.6
  783.8 1.6 copy.174
  785.4 1.6 convolution_add_fusion.4
  787.0 6.6 copy.135
  793.5 5.8 reshape.212
  799.3 5.3 all-to-all-start
  805.0 6.7 copy.129
  811.7 41.7 %all-to-all-done = f32[2,512,1024]{2,0,1:T(2,128)} async-done(((f32[2,512,1024]{2,0,1:T(2,128)}), f32[2,512,1024]{2,0,1:T(2,128)}, u32[]{:S(2)}, u32[]{:S(2)}) %all-to-all-start) | async-done | bytes 4194336 | tf_op jit(solution)/shard_map/all_to_all | solution.py:110
  853.4 3.5 copy.125
  856.9 1.9 copy-done.3
  858.8 2.9 mul.258
  861.7 5.4 copy.126
  867.1 5.4 copy.127
  872.5 2.7 reduce_sum.38
  875.2 4.3 fusion.28
  880.1 2.7 copy.130
  882.8 6.3 psum.7
  (87 shorter events, 5.2 us)
Async XLA Ops:
  7.2 797.8 %copy-start = (f32[128]{0:T(128)S(1)}, f32[128]{0:T(128)}, u32[]{:S(2)}) copy-start(f32[128]{0:T(128)} %param.28) | copy-start | bytes 1540
  7.2 718.9 %all-gather.2.cloned.1.call-start = ((), (), s32[]{:S(2)}) async-start(), calls=%async_computation.2 | async-start | bytes 1310720 | tf_op jit(solution)/shard_map/all_gather | solution.py:150
  7.9 9.9 %copy-start.9 = (f32[4,2,512]{2,1,0:T(2,128)S(1)}, f32[4,2,512]{2,1,0:T(2,128)}, u32[]{:S(2)}) copy-start(f32[4,2,512]{2,1,0:T(2,128)} %param.23) | copy-start | bytes 49156
  13.0 786.3 %all-to-all-start.1 = ((bf16[2,512,1024]{2,0,1:T(2,128)(2,1)}), bf16[2,512,1024]{2,0,1:T(2,128)(2,1)}, u32[]{:S(2)}, u32[]{:S(2)}) async-start(bf16[2,512,1024]{2,0,1:T(2,128)(2,1)} %copy.128), calls=%async_computation.1 | async-start | bytes 4194304 | tf_op jit(solution)/shard_map/all_to_all | solution.py:111
  29.8 1.6 copy-start.10
  29.8 1.6 copy-start.6
  34.2 3.0 copy-start.15
  34.2 3.0 copy-start.7
  34.2 3.0 copy-start.8
  34.2 3.0 copy-start.13
  40.1 2.0 copy-start.1
  689.4 2.0 copy-start.4
  709.1 5.3 copy-start.2
  709.1 6.4 copy-start.5
  715.5 10.6 %copy-start.14 = (s32[2]{0:T(128)S(1)}, s32[2]{0:T(128)}, u32[]{:S(2)}) copy-start(s32[2]{0:T(128)} %param.26) | copy-start | bytes 28
  799.3 5.3 copy-start.11
  799.3 5.4 copy-start.12
  799.3 54.0 %all-to-all-start = ((f32[2,512,1024]{2,0,1:T(2,128)}), f32[2,512,1024]{2,0,1:T(2,128)}, u32[]{:S(2)}, u32[]{:S(2)}) async-start(f32[2,512,1024]{2,0,1:T(2,128)} %reshape.212), calls=%async_computation | async-start | bytes 8388608 | tf_op jit(solution)/shard_map/all_to_all | solution.py:110
  856.9 1.9 copy-start.3
Sparse Core Ops, SparseCore 0:
  9.6 30.6 all-gather.1
where the time goes:
time: 900 us; the launch traced here: 896 us
  other arithmetic  660 us (73%)
  local copies, waits for them, and re-layouts  87.1 us (10%)
  matrix products  75.6 us (8%)
  waiting for transfers between devices  42.4 us (5%)
  between operations  14.8 us (2%)
  starting transfers between devices  10.1 us (1%)
    another operation x2, other arithmetic, delta_blocks(): jax.scipy.linalg.solve_triangular(system, right, lower=True, unit_diagona...  630 us
    all_to_all x1, waiting for transfers between devices, shuffle_pair(): lax.all_to_all(core, ('head', 'sub'), split_axis=1, concat_axis=2, tiled=...  41.7 us
  transfers between devices with their start and end apart: 3, of which 1 were waited for; matrix products, arithmetic and copies ran while one was open for 88% of the time, Pallas kernels for 0%

commit v1 on v0

--- a/solution.py
+++ b/solution.py
@@ -4,6 +4,12 @@
 from jax.sharding import PartitionSpec as P
 
 BLOCK = 128
+_post_paths = lambda raw, device_axis: jnp.concatenate(
+    jax.lax.all_to_all(
+        jnp.stack(jnp.split(raw, jax.lax.axis_size(device_axis), axis=1)), device_axis, 0, 0
+    ),
+    2,
+)
 
 
 def conv_silu(inputs, kernel):
@@ -107,7 +113,7 @@
 
 def shuffle_pair(core, gate):
     moved_core, moved_gate = (
-        lax.all_to_all(core, ("head", "sub"), split_axis=1, concat_axis=2, tiled=True),
+        _post_paths(core, ("head", "sub")),
         lax.all_to_all(
             gate.astype(jnp.float32), ("head", "sub"), split_axis=1, concat_axis=2, tiled=True
         ).astype(gate.dtype),

time: 900 us -> 901 us (level)
  no operation moved by 1% of the time
where the time goes in v1:
time: 901 us; the launch traced here: 896 us
  other arithmetic  664 us (74%)
  local copies, waits for them, and re-layouts  83.1 us (9%)
  matrix products  75.6 us (8%)
  waiting for transfers between devices  42.4 us (5%)
  between operations  14.8 us (2%)
  starting transfers between devices  9.99 us (1%)
    another operation x2, other arithmetic, delta_blocks(): jax.scipy.linalg.solve_triangular(system, right, lower=True, unit_diagona...  630 us
    all_to_all x1, waiting for transfers between devices, jax.lax.all_to_all(jnp.stack(jnp.split(raw, jax.lax.axis_size(device_axis...  41.7 us
  transfers between devices with their start and end apart: 3, of which 1 were waited for; matrix products, arithmetic and copies ran while one was open for 88% of the time, Pallas kernels for 0%

profile of v1, /device:TPU:0, one launch (start us, length us, event | category | flops | bytes accessed | tf_op | source)
XLA Modules:
  0.0 896.5 jit_solution(10230409666183119312)
XLA Ops:
  7.9 5.1 copy.125
  13.0 4.8 all-to-all-start.1
  17.9 3.3 reshape.200
  21.2 2.8 divide_multiply_fusion.1
  24.0 2.6 fusion.49
  26.5 1.9 reshape.201
  28.5 1.2 multiply_reduce_fusion.1
  29.8 1.4 broadcast_divide_fusion
  31.4 2.8 divide_multiply_fusion
  34.2 2.9 copy.138
  37.3 2.3 reduce_window_sum.11
  40.1 1.9 copy-done.1
  42.1 11.1 %add_bitcast_fusion = f32[4,2,8,1,128,128]{5,4,3,2,1,0:T(8,128)} fusion(f32[128,128]{1,0:T(8,128)S(1)} %get-tuple-element.153, f32[4,2,8,128]{3,2,1,0:T(8,128)S(1)} %reduce_window_sum.11, f32[4,2,8,128]{3,2,1,0:T(8,128)S(1)} %copy_bitcast_fusion, f32[128,128]{1,0:T(8,128)S(1)} %get-tuple-element.152, pred[128,128]{1,0:T(8,128)(4,1)S(1)} %iota_compare_fusion.1, ...), kind=kOutput, calls=%fused_computation.45 | convolution fusion | flops 1620049920 | bytes 8634368 | tf_op jit(solution)/shard_map/nshid,nshjd->nshij/dot_general | solution.py:58
  53.2 630.3 %custom-call.4 = f32[4,2,8,1,128,128]{4,5,3,2,1,0:T(8,128)} custom-call(f32[4,2,8,1,128,128]{5,4,3,2,1,0:T(8,128)} %add_bitcast_fusion), custom_call_target="InvertDiagBlocksLowerTriangular" | custom-call | tf_op jit(solution)/shard_map/jit(_solve_triangular)/vmap(vmap(vmap()))/triangular_solve | solution.py:66
  683.5 2.4 reshape.203
  685.9 1.2 multiply_reduce_fusion
  687.2 1.5 divide_multiply_fusion.2
  689.4 2.0 copy-done.3
  691.4 2.2 copy.121
  693.6 5.2 bitcast_multiply_fusion.3
  698.8 10.3 %fusion.12 = f32[4,2,8,128,256]{4,3,2,1,0:T(8,128)S(1)} fusion(f32[4,2,8,128,128]{4,3,2,1,0:T(8,128)S(1)} %get-tuple-element.155, f32[4,2,8,128,128]{4,3,2,1,0:T(8,128)S(1)} %get-tuple-element.154, f32[4,2,8,1,128,128]{4,5,3,2,1,0:T(8,128)} %custom-call.4), kind=kOutput, calls=%fused_computation.23 | convolution fusion | flops 3223322624 | bytes 20971520 | tf_op jit(solution)/shard_map/jit(_solve_triangular)/vmap(vmap(vmap()))/triangular_solve | solution.py:66
  709.1 5.3 fusion.48
  714.4 1.1 copy-done.4
  715.5 10.6 %fusion.27 = f32[4,2,8,128,128]{4,3,2,1,0:T(8,128)} fusion(f32[4,2,8,128]{3,2,1,0:T(8,128)S(1)} %reduce_window_sum.11, pred[128,128]{1,0:T(8,128)(4,1)S(1)} %iota_compare_fusion.1, f32[2,4,128,8,128]{4,2,1,3,0:T(8,128)S(1)} %bitcast.185, f32[4,2,8,128,128]{4,3,0,2,1:T(8,128)S(1)} %bitcast.187), kind=kOutput, calls=%fused_computation.47 | convolution fusion | flops 1614807040 | bytes 12632064 | tf_op jit(solution)/shard_map/nshid,nshjd->nshij/dot_general | solution.py:69
  726.1 2.2 fusion.35
  728.4 58.6 %while.13 = (s32[]{:T(128)}, f32[2,8,128,128]{3,2,1,0:T(8,128)S(1)}, f32[4,2,8,128,128]{4,3,2,1,0:T(8,128)}, f32[4,2,8,128]{3,2,1,0:T(8,128)S(1)}, f32[4,2,8,128...) while((s32[]{:T(128)}, ...), condition=%wide.region_4.5_spmd.clone, body=%wide.region_3.4_spmd.sunk.clone | while | flops 1612187648 | bytes 20032420 | solution.py:85
  728.8 2.5 convolution_multiply_fusion.3
  731.3 2.8 convolution_subtract_fusion.3
  734.1 3.4 fusion.82
  737.6 2.3 constant_dynamic-slice_fusion.6
  739.9 1.6 copy.169
  741.5 1.6 convolution_add_fusion.4
  743.4 2.5 convolution_multiply_fusion.3
  745.9 2.8 convolution_subtract_fusion.3
  748.7 3.4 fusion.82
  752.2 2.3 constant_dynamic-slice_fusion.6
  754.5 1.6 copy.169
  756.1 1.6 convolution_add_fusion.4
  758.1 2.5 convolution_multiply_fusion.3
  760.6 2.8 convolution_subtract_fusion.3
  763.4 3.4 fusion.82
  766.8 2.3 constant_dynamic-slice_fusion.6
  769.2 1.6 copy.169
  770.7 1.6 convolution_add_fusion.4
  772.7 2.5 convolution_multiply_fusion.3
  775.2 2.8 convolution_subtract_fusion.3
  778.0 3.4 fusion.82
  781.5 2.3 constant_dynamic-slice_fusion.6
  783.8 1.6 copy.169
  785.4 1.6 convolution_add_fusion.4
  787.0 6.5 copy.122
  793.5 4.9 reshape.204
  798.4 2.5 slice_bitcast_fusion.4
  800.9 2.3 pad_maximum_fusion
  803.2 5.2 all-to-all-start
  808.7 6.8 copy.126
  815.5 41.7 %all-to-all-done = f32[4,2,128,1024]{3,2,1,0:T(8,128)} async-done(((f32[4,2,128,1024]{3,2,1,0:T(8,128)}), f32[4,2,128,1024]{3,2,1,0:T(8,128)}, u32[]{:S(2)}, u32[]{:S(2)}) %all-to-all-start) | async-done | bytes 4194336 | tf_op jit(solution)/shard_map/all_to_all | solution.py:8
  857.2 5.0 bitcast_multiply_fusion.5
  862.1 5.4 copy.124
  867.5 2.7 reduce_sum.38
  870.2 5.4 copy.123
  875.6 4.3 fusion.28
  880.4 2.7 copy.127
  883.1 6.3 psum.7
  (86 shorter events, 5.2 us)
Async XLA Ops:
  7.2 801.5 %copy-start = (f32[128]{0:T(128)S(1)}, f32[128]{0:T(128)}, u32[]{:S(2)}) copy-start(f32[128]{0:T(128)} %param.28) | copy-start | bytes 1540
  7.2 718.9 %all-gather.2.cloned.1.call-start = ((), (), s32[]{:S(2)}) async-start(), calls=%async_computation.2 | async-start | bytes 1310720 | tf_op jit(solution)/shard_map/all_gather | solution.py:156
  7.9 9.9 %copy-start.8 = (f32[4,2,512]{2,1,0:T(2,128)S(1)}, f32[4,2,512]{2,1,0:T(2,128)}, u32[]{:S(2)}) copy-start(f32[4,2,512]{2,1,0:T(2,128)} %param.23) | copy-start | bytes 49156
  13.0 790.2 %all-to-all-start.1 = ((bf16[2,512,1024]{2,0,1:T(2,128)(2,1)}), bf16[2,512,1024]{2,0,1:T(2,128)(2,1)}, u32[]{:S(2)}, u32[]{:S(2)}) async-start(bf16[2,512,1024]{2,0,1:T(2,128)(2,1)} %copy.125), calls=%async_computation.1 | async-start | bytes 4194304 | tf_op jit(solution)/shard_map/all_to_all | solution.py:117
  29.8 1.6 copy-start.9
  29.8 1.6 copy-start.5
  34.2 3.0 copy-start.14
  34.2 3.0 copy-start.6
  34.2 3.0 copy-start.7
  34.2 3.0 copy-start.12
  40.1 2.0 copy-start.1
  689.4 2.0 copy-start.3
  709.1 5.3 copy-start.2
  709.1 6.4 copy-start.4
  715.5 10.6 %copy-start.13 = (s32[2]{0:T(128)S(1)}, s32[2]{0:T(128)}, u32[]{:S(2)}) copy-start(s32[2]{0:T(128)} %param.26) | copy-start | bytes 28
  803.1 5.2 copy-start.10
  803.1 5.3 copy-start.11
  803.2 54.0 %all-to-all-start = ((f32[4,2,128,1024]{3,2,1,0:T(8,128)}), f32[4,2,128,1024]{3,2,1,0:T(8,128)}, u32[]{:S(2)}, u32[]{:S(2)}) async-start(f32[4,2,128,1024]{3,2,1,0:T(8,128)} %pad_maximum_fusion), calls=%async_computation | async-start | bytes 8388608 | tf_op jit(solution)/shard_map/all_to_all | solution.py:8
Sparse Core Ops, SparseCore 0:
  9.6 30.6 all-gather.1
